TPU v7x, 128 devices: a whole 4x4x4 slice. The times are simulated.
128 devices in a mesh: dp: 16 (over z, y), ctx: 2 (over x_hi), tp: 4 (over x_lo, core).
Axes of the slice: x: 4 (x_hi: 2, x_lo: 2; x = x_hi * 2 + x_lo), y: 4, z: 4, core: 2. Of those that a mesh axis runs over, the one named last changes fastest.
Arguments:
- stream: bfloat16 [16, 2048, 768], P('dp', 'ctx'), may hold values from -6 to 6
- norm_gain: bfloat16 [768], P('dp'), may hold values from 0.5 to 1.5
- w_gate: bfloat16 [768, 1536], P('dp', 'tp'), may hold values from -0.21875 to 0.21875
- w_value: bfloat16 [768, 1536], P('dp', 'tp'), may hold values from -0.21875 to 0.21875
- w_step: bfloat16 [768, 24], P('dp', 'tp'), may hold values from -0.21875 to 0.21875
- w_state: bfloat16 [768, 256], P('dp'), may hold values from -0.21875 to 0.21875
- w_out: bfloat16 [1536, 768], P('tp', 'dp'), may hold values from -0.15625 to 0.15625
- conv_value: float32 [4, 1536], P(None, 'tp'), may hold values from -3 to 3
- conv_value_bias: float32 [1536], P('tp'), may hold values from -3 to 3
- conv_state: float32 [4, 256], replicated, may hold values from -3 to 3
- conv_state_bias: float32 [256], replicated, may hold values from -3 to 3
- step_bias: float32 [24], P('tp'), may hold values from -5 to -1
- decay_log: float32 [24], P('tp'), may hold values from -5 to 0.5
- skip_gain: float32 [24], P('tp'), may hold values from 0.5 to 1.5
- inner_gain: float32 [1536], P('tp'), may hold values from 0.5 to 1.5
- cotangent: bfloat16 [16, 2048, 768], P('dp', 'ctx'), may hold values from -6 to 6
Outputs:
- mixed_out: bfloat16 [16, 2048, 768], P('dp', 'ctx')
- d_stream: float32 [16, 2048, 768], P('dp', 'ctx')
- grad_norm_gain: float32 [768], P('dp')
- grad_w_gate: float32 [768, 1536], P('dp', 'tp')
- grad_w_value: float32 [768, 1536], P('dp', 'tp')
- grad_w_step: float32 [768, 24], P('dp', 'tp')
- grad_w_state: float32 [768, 256], P('dp')
- grad_w_out: float32 [1536, 768], P('tp', 'dp')
- grad_conv_value: float32 [4, 1536], P(None, 'tp')
- grad_conv_value_bias: float32 [1536], P('tp')
- grad_conv_state: float32 [4, 256], replicated
- grad_conv_state_bias: float32 [256], replicated
- grad_step_bias: float32 [24], P('tp')
- grad_decay_log: float32 [24], P('tp')
- grad_skip_gain: float32 [24], P('tp')
- grad_inner_gain: float32 [1536], P('tp')
All inputs are finite; a program needn't handle non-finite values.
Results may differ from a plain program's by a relative error of at most 0.0095.
The roundings to bfloat16 on the way count: a program that leaves them out, or rounds other values in their place, can miss the bound.
Values may be sent and summed in bfloat16 or wider, within the bound.
A program may use at most 128 MiB of HBM per device.

v0:
```python
import jax
import jax.numpy as jnp
from jax import lax
from jax.sharding import PartitionSpec as P

D = 768
HEAD = 64
STATE = 128
CONV = 4
GROUP = 256
INNER = 1536


EPS = 1e-05
HIGH = lax.Precision.HIGHEST


def passed_along(value, axis, steps):
    count = lax.axis_size(axis)
    initial, last = (max(0, -steps), min(count, count - steps))
    return lax.ppermute(value, axis, [(source, source + steps) for source in range(initial, last)])


def prefix(value, axis, join, neutral, backward):
    count, mine = (lax.axis_size(axis), lax.axis_index(axis))
    pieces = jax.tree.map(lambda part: lax.all_gather(part, axis), value)
    if backward:
        pieces = jax.tree.map(lambda part: part[::-1], pieces)
        mine = count - 1 - mine
    so_far = jax.tree.map(
        lambda part, zero: jnp.full_like(part, 0) + jnp.asarray(zero, part.dtype), value, neutral
    )

    def hop(position, so_far):
        longer = join(so_far, jax.tree.map(lambda part: part[position], pieces))
        return jax.tree.map(lambda new, old: jnp.where(position < mine, new, old), longer, so_far)

    return lax.fori_loop(0, count - 1, hop, so_far)


def matmul(left, right):
    return jnp.dot(left, right, preferred_element_type=jnp.float32)


def back_matmul(grad_rows, weight):
    return lax.dot_general(
        grad_rows, weight, (((1,), (1,)), ((), ())), preferred_element_type=jnp.float32
    )


def silu_grad(pre_act):
    sigmoid_val = jax.nn.sigmoid(pre_act)
    return sigmoid_val * (1.0 + pre_act * (1.0 - sigmoid_val))


def link_pairs(earlier, later_pair):
    return (earlier[0] * later_pair[0], later_pair[0][:, None, None] * earlier[1] + later_pair[1])


def chain_step(carry_in, pieces):
    decay_now, fresh_now = pieces
    return (decay_now[:, None, None] * carry_in + fresh_now, carry_in)


def per_device(
    stream,
    norm_gain,
    w_gate,
    w_value,
    w_step,
    w_state,
    w_out,
    conv_value,
    conv_value_bias,
    conv_state,
    conv_state_bias,
    step_bias,
    decay_log,
    skip_gain,
    inner_gain,
    cotangent,
):
    tokens = stream.shape[1]
    local_heads = step_bias.shape[0]
    local_inner = inner_gain.shape[0]
    blocks = tokens // GROUP
    bfloat = jnp.bfloat16
    gain_full, gate_full, value_full, step_full, state_full, out_full = (
        lax.all_gather(norm_gain, "dp", axis=0, tiled=True),
        lax.all_gather(w_gate, "dp", axis=0, tiled=True),
        lax.all_gather(w_value, "dp", axis=0, tiled=True),
        lax.all_gather(w_step, "dp", axis=0, tiled=True),
        lax.all_gather(w_state, "dp", axis=0, tiled=True),
        lax.all_gather(w_out, "dp", axis=1, tiled=True),
    )
    source = stream[0].astype(jnp.float32)
    scale_zero = lax.rsqrt(jnp.mean(source * source, axis=-1, keepdims=True) + EPS)
    gain_zero = gain_full.astype(jnp.float32)
    normed = (source * scale_zero * gain_zero).astype(bfloat)
    gate_out = matmul(normed, gate_full)
    value_pre = matmul(normed, value_full).astype(bfloat)
    state_pre = matmul(normed, state_full).astype(bfloat)
    step_raw = matmul(normed, step_full)
    conv_input = jnp.concatenate([value_pre, state_pre], axis=1)
    edge_rows = passed_along(conv_input[tokens - (CONV - 1) :], "ctx", 1)
    padded = jnp.concatenate([edge_rows, conv_input], axis=0).astype(jnp.float32)
    kernel = jnp.concatenate([conv_value, conv_state], axis=1)
    kernel_bias = jnp.concatenate([conv_value_bias, conv_state_bias])
    conv_sum = kernel_bias + sum(
        (kernel[offset] * padded[offset : offset + tokens] for offset in range(CONV))
    )
    activated = jax.nn.silu(conv_sum)
    values = activated[:, :local_inner].astype(bfloat).reshape(blocks, GROUP, local_heads, HEAD)
    keys_low = (
        activated[:, local_inner : local_inner + STATE].astype(bfloat).reshape(blocks, GROUP, STATE)
    )
    reads_low = activated[:, local_inner + STATE :].astype(bfloat).reshape(blocks, GROUP, STATE)
    step_val = jax.nn.softplus(step_raw + step_bias)
    decay_rate = jnp.exp(decay_log)
    log_rate = -decay_rate * step_val
    step_blocks = step_val.reshape(blocks, GROUP, local_heads).transpose(0, 2, 1)
    cum_log = jnp.cumsum(log_rate.reshape(blocks, GROUP, local_heads), axis=1).transpose(0, 2, 1)
    last_cum = cum_log[:, :, -1]
    lower_mask = jnp.arange(GROUP)[:, None] >= jnp.arange(GROUP)[None, :]
    decays = jnp.exp(jnp.where(lower_mask, cum_log[:, :, :, None] - cum_log[:, :, None, :], -1e30))
    inner_prod = jnp.einsum("ctn,csn->cts", reads_low, keys_low, preferred_element_type=jnp.float32)
    weights = inner_prod[:, None] * decays * step_blocks[:, :, None, :]
    weights_low = weights.astype(bfloat)
    local_out = jnp.einsum(
        "chts,cshp->cthp", weights_low, values, preferred_element_type=jnp.float32
    )
    scales = step_blocks * jnp.exp(last_cum[:, :, None] - cum_log)
    scales_t = scales.transpose(0, 2, 1)
    values_f = values.astype(jnp.float32)
    weighted = (values_f * scales_t[..., None]).astype(bfloat)
    fresh_state = jnp.einsum(
        "cshp,csn->chpn", weighted, keys_low, preferred_element_type=jnp.float32
    )
    block_decay = jnp.exp(last_cum)
    zero_state = jnp.zeros((local_heads, HEAD, STATE), jnp.float32)
    device_state, unused = lax.scan(chain_step, zero_state, (block_decay, fresh_state))
    device_decay = jnp.prod(block_decay, axis=0)
    identity = (jnp.ones((local_heads,), jnp.float32), zero_state)
    entering = prefix((device_decay, device_state), "ctx", link_pairs, identity, False)[1]
    unused, states_in = lax.scan(chain_step, entering, (block_decay, fresh_state))
    states_low = states_in.astype(bfloat)
    carried_pre = jnp.einsum(
        "ctn,chpn->cthp", reads_low, states_low, preferred_element_type=jnp.float32
    )
    exp_cum = jnp.exp(cum_log).transpose(0, 2, 1)
    ssd_heads = (
        local_out + exp_cum[..., None] * carried_pre + skip_gain[None, None, :, None] * values_f
    )
    ssd_out = ssd_heads.reshape(tokens, local_inner)
    gate_act = jax.nn.silu(gate_out)
    gated = ssd_out * gate_act
    square_sum = lax.psum(jnp.sum(gated * gated, axis=1), "tp")
    scale_one = lax.rsqrt(square_sum / INNER + EPS)[:, None]
    normal_out = (gated * scale_one * inner_gain).astype(bfloat)
    branch = lax.psum(matmul(normal_out, out_full), "tp")
    mixed_out = (source + branch).astype(bfloat)[None]
    upstream = cotangent[0]
    grad_w_out = matmul(normal_out.T, upstream)
    grad_normal = back_matmul(upstream, out_full)
    grad_inner_gain = jnp.sum(grad_normal * gated * scale_one, axis=0)
    scaled_grad = grad_normal * inner_gain
    cross_sum = lax.psum(jnp.sum(scaled_grad * gated, axis=1), "tp")
    grad_gated = (
        scale_one * scaled_grad
        - gated * (scale_one * scale_one * scale_one) * (cross_sum / INNER)[:, None]
    )
    grad_ssd = (grad_gated * gate_act).astype(bfloat)
    grad_gate = (grad_gated * ssd_out * silu_grad(gate_out)).astype(bfloat)
    grad_heads = grad_ssd.reshape(blocks, GROUP, local_heads, HEAD)
    grad_heads_f = grad_heads.astype(jnp.float32)
    grad_skip_gain = jnp.sum(grad_heads_f * values_f, axis=(0, 1, 3))
    grad_values = skip_gain[None, None, :, None] * grad_heads_f
    grad_weights = jnp.einsum(
        "cthp,cshp->chts", grad_heads, values, preferred_element_type=jnp.float32
    )
    grad_values = grad_values + jnp.einsum(
        "chts,cthp->cshp", weights_low, grad_heads, preferred_element_type=jnp.float32
    )
    product = grad_weights * weights
    grad_cum = jnp.sum(product, axis=3) - jnp.sum(product, axis=2)
    grad_step = jnp.sum(grad_weights * inner_prod[:, None] * decays, axis=2)
    grad_inner = jnp.sum(grad_weights * decays * step_blocks[:, :, None, :], axis=1)
    grad_exp = grad_heads_f * exp_cum[..., None]
    grad_carried = grad_exp.astype(bfloat)
    grad_cum = grad_cum + jnp.sum(grad_exp * carried_pre, axis=3).transpose(0, 2, 1)
    grad_reads = jnp.einsum(
        "cthp,chpn->ctn", grad_carried, states_low, preferred_element_type=jnp.float32
    )
    grad_state_read = jnp.einsum(
        "cthp,ctn->chpn", grad_carried, reads_low, preferred_element_type=jnp.float32
    )
    local_in, unused = lax.scan(
        chain_step, zero_state, (block_decay, grad_state_read), reverse=True
    )
    arriving = prefix((device_decay, local_in), "ctx", link_pairs, identity, True)[1]
    unused, grad_state_out = lax.scan(
        chain_step, arriving, (block_decay, grad_state_read), reverse=True
    )
    grad_last = jnp.sum(grad_state_out * states_in, axis=(2, 3)) * block_decay
    grad_fresh = grad_state_out.astype(bfloat)
    grad_weighted = jnp.einsum(
        "csn,chpn->cshp", keys_low, grad_fresh, preferred_element_type=jnp.float32
    )
    grad_keys = jnp.einsum(
        "cshp,chpn->csn", weighted, grad_fresh, preferred_element_type=jnp.float32
    )
    grad_values = grad_values + grad_weighted * scales_t[..., None]
    grad_scales = jnp.sum(grad_weighted * values_f, axis=3).transpose(0, 2, 1)
    grad_step = grad_step + grad_scales * jnp.exp(last_cum[:, :, None] - cum_log)
    spill_term = grad_scales * scales
    grad_last = grad_last + jnp.sum(spill_term, axis=2)
    last_flag = (jnp.arange(GROUP) == GROUP - 1).astype(jnp.float32)
    grad_cum = grad_cum - spill_term + grad_last[:, :, None] * last_flag
    keys_f = keys_low.astype(jnp.float32)
    reads_f = reads_low.astype(jnp.float32)
    grad_reads = grad_reads + jnp.einsum("cts,csn->ctn", grad_inner, keys_f, precision=HIGH)
    grad_keys = grad_keys + jnp.einsum("cts,ctn->csn", grad_inner, reads_f, precision=HIGH)
    grad_rate = lax.cumsum(grad_cum, axis=2, reverse=True)
    grad_step = grad_step - decay_rate[None, :, None] * grad_rate
    grad_decay_log = -decay_rate * jnp.sum(grad_rate * step_blocks, axis=(0, 2))
    grad_step_pre = grad_step.transpose(0, 2, 1).reshape(tokens, local_heads) * jax.nn.sigmoid(
        step_raw + step_bias
    )
    grad_step_bias = jnp.sum(grad_step_pre, axis=0)
    grad_step_low = grad_step_pre.astype(bfloat)
    state_grads = jnp.concatenate(
        [grad_keys.reshape(tokens, STATE), grad_reads.reshape(tokens, STATE)], axis=1
    )
    state_grads = lax.psum(state_grads, "tp")
    grad_act = jnp.concatenate([grad_values.reshape(tokens, local_inner), state_grads], axis=1)
    grad_conv = grad_act * silu_grad(conv_sum)
    grad_padded = sum(
        (
            jnp.pad(kernel[offset] * grad_conv, ((offset, CONV - 1 - offset), (0, 0)))
            for offset in range(CONV)
        )
    )
    incoming = passed_along(grad_padded[: CONV - 1], "ctx", -1)
    grad_input = grad_padded[CONV - 1 :] + jnp.pad(incoming, ((tokens - (CONV - 1), 0), (0, 0)))
    grad_kernel = jnp.stack(
        [jnp.sum(grad_conv * padded[offset : offset + tokens], axis=0) for offset in range(CONV)]
    )
    grad_kernel_bias = jnp.sum(grad_conv, axis=0)
    grad_value_low = grad_input[:, :local_inner].astype(bfloat)
    grad_state_low = grad_input[:, local_inner:].astype(bfloat)
    normed_t = normed.T
    grad_w_gate = matmul(normed_t, grad_gate)
    grad_w_value = matmul(normed_t, grad_value_low)
    grad_w_step = matmul(normed_t, grad_step_low)
    grad_w_state = matmul(normed_t, grad_state_low)
    partial_normed = (
        back_matmul(grad_gate, gate_full)
        + back_matmul(grad_value_low, value_full)
        + back_matmul(grad_step_low, step_full)
    )
    grad_normed = lax.psum(partial_normed, "tp") + back_matmul(grad_state_low, state_full)
    grad_norm_gain = jnp.sum(grad_normed * source * scale_zero, axis=0)
    scaled_zero = grad_normed * gain_zero
    grad_source = scale_zero * scaled_zero - source * (scale_zero * scale_zero * scale_zero) * (
        jnp.sum(scaled_zero * source, axis=1, keepdims=True) / D
    )
    d_stream = (upstream.astype(jnp.float32) + grad_source)[None]
    grad_conv_value = grad_kernel[:, :local_inner]
    grad_conv_value_bias = grad_kernel_bias[:local_inner]
    grad_conv_state = grad_kernel[:, local_inner:]
    grad_conv_state_bias = grad_kernel_bias[local_inner:]
    pieces_out = (
        lax.psum_scatter(grad_norm_gain, ("dp", "ctx"), scatter_dimension=0, tiled=True),
        lax.psum_scatter(grad_w_gate, ("dp", "ctx"), scatter_dimension=0, tiled=True),
        lax.psum_scatter(grad_w_value, ("dp", "ctx"), scatter_dimension=0, tiled=True),
        lax.psum_scatter(grad_w_step, ("dp", "ctx"), scatter_dimension=0, tiled=True),
        lax.psum_scatter(grad_w_state, ("dp", "ctx"), scatter_dimension=0, tiled=True),
        lax.psum_scatter(grad_w_out, ("dp", "ctx"), scatter_dimension=1, tiled=True),
    )
    owned_part = (
        lax.all_gather(pieces_out[0], "ctx", axis=0, tiled=True),
        lax.all_gather(pieces_out[1], "ctx", axis=0, tiled=True),
        lax.all_gather(pieces_out[2], "ctx", axis=0, tiled=True),
        lax.all_gather(pieces_out[3], "ctx", axis=0, tiled=True),
        lax.all_gather(pieces_out[4], "ctx", axis=0, tiled=True),
        lax.all_gather(pieces_out[5], "ctx", axis=1, tiled=True),
    )
    small_sum = lax.psum(
        (
            grad_conv_value,
            grad_conv_value_bias,
            grad_conv_state,
            grad_conv_state_bias,
            grad_step_bias,
            grad_decay_log,
            grad_skip_gain,
            grad_inner_gain,
        ),
        ("dp", "ctx"),
    )
    return (
        mixed_out,
        d_stream,
        owned_part[0],
        owned_part[1],
        owned_part[2],
        owned_part[3],
        owned_part[4],
        owned_part[5],
        small_sum[0],
        small_sum[1],
        small_sum[2],
        small_sum[3],
        small_sum[4],
        small_sum[5],
        small_sum[6],
        small_sum[7],
    )


def solution(mesh):
    in_specs = (
        P("dp", "ctx", None),
        P("dp"),
        P("dp", "tp"),
        P("dp", "tp"),
        P("dp", "tp"),
        P("dp", None),
        P("tp", "dp"),
        P(None, "tp"),
        P("tp"),
        P(),
        P(),
        P("tp"),
        P("tp"),
        P("tp"),
        P("tp"),
        P("dp", "ctx", None),
    )
    out_specs = (
        P("dp", "ctx", None),
        P("dp", "ctx", None),
        P("dp"),
        P("dp", "tp"),
        P("dp", "tp"),
        P("dp", "tp"),
        P("dp", None),
        P("tp", "dp"),
        P(None, "tp"),
        P("tp"),
        P(),
        P(),
        P("tp"),
        P("tp"),
        P("tp"),
        P("tp"),
    )
    return jax.shard_map(
        per_device, mesh=mesh, in_specs=in_specs, out_specs=out_specs, check_vma=False
    )
```

profile of v0, /device:TPU:0, one launch (start us, length us, event | category | flops | bytes accessed | tf_op | source)
XLA Modules:
  0.0 1505.7 jit_solution(11385496539851502870)
XLA Ops:
  10.8 42.0 %all-reduce.5 = bf16[768]{0:T(1024)(128)(2,1)S(1)} all-reduce(bf16[768]{0:T(1024)(128)(2,1)S(1)} %dynamic-update-slice), channel_id=1, replica_groups=mesh['dp'=16,'ctx'=2,'tp'=4] {'dp'}, use_global_device_ids=true, to_apply=%add.5 | all-reduce | flops 768 | bytes 3072
  52.9 1.9 fusion.6
  55.4 21.1 %all_gather.57 = bf16[768,384]{1,0:T(8,128)(2,1)S(1)} all-gather(bf16[48,384]{1,0:T(8,128)(2,1)S(1)} %copy-done.56), channel_id=1, replica_groups=mesh['dp'=16,'ctx'=2,'tp'=4] {'dp'}, dimensions={0}, use_global_device_ids=true | all-gather | bytes 626688 | tf_op jit(solution)/shard_map/all_gather | solution.py:91
  76.5 24.1 %all_gather.58 = bf16[768,256]{1,0:T(8,128)(2,1)S(1)} all-gather(bf16[48,256]{1,0:T(8,128)(2,1)S(1)} %copy-done.66), channel_id=1, replica_groups=mesh['dp'=16,'ctx'=2,'tp'=4] {'dp'}, dimensions={0}, use_global_device_ids=true | all-gather | bytes 417792 | tf_op jit(solution)/shard_map/all_gather | solution.py:93
  102.8 5.7 collective-permute-start
  108.5 20.4 %all-gather.3 = bf16[16,48,6]{1,2,0:T(8,128)(2,1)S(1)} all-gather(bf16[1,48,6]{1,2,0:T(8,128)(2,1)S(1)} %bitcast.219), channel_id=1, replica_groups=mesh['dp'=16,'ctx'=2,'tp'=4] {'dp'}, dimensions={0}, use_global_device_ids=true | all-gather | bytes 9792 | tf_op jit(solution)/shard_map/all_gather | solution.py:92
  130.8 7.2 reduce-window.14
  141.0 6.4 all-reduce.6
  148.0 26.2 %all_gather.64 = bf16[768,384]{1,0:T(8,128)(2,1)} all-gather(bf16[48,384]{1,0:T(8,128)(2,1)S(1)} %copy-done.57), channel_id=1, replica_groups=mesh['dp'=16,'ctx'=2,'tp'=4] {'dp'}, dimensions={0}, use_global_device_ids=true | all-gather | bytes 626688 | tf_op jit(solution)/shard_map/all_gather | solution.py:90
  174.1 23.7 %all_gather.65 = bf16[384,768]{0,1:T(8,128)(2,1)} all-gather(bf16[384,48]{0,1:T(8,128)(2,1)S(1)} %copy-done.58), channel_id=1, replica_groups=mesh['dp'=16,'ctx'=2,'tp'=4] {'dp'}, dimensions={1}, use_global_device_ids=true | all-gather | bytes 626688 | tf_op jit(solution)/shard_map/all_gather | solution.py:94
  198.5 1.9 maximum_convert_fusion
  200.5 3.9 multiply_convert_fusion
  206.7 2.6 reshape.164
  209.3 1.8 reshape.166
  213.0 1.8 copy.256
  214.8 2.5 fusion.44
  217.3 4.2 while.66
  221.5 8.0 all-gather.1
  230.6 7.0 while.64
  237.5 1.8 reshape.165
  239.4 1.8 copy.211
  241.2 1.8 copy.257
  245.2 2.1 fusion.28
  250.4 2.7 multiply_reduce_fusion.9
  253.1 6.0 psum.91
  259.1 4.7 multiply_reduce_fusion.6
  263.7 5.7 psum.93
  269.5 6.0 multiply_reduce_fusion.7
  275.5 2.6 reshape.172
  278.1 2.6 fusion.47
  280.7 6.9 fusion.4
  288.9 4.2 while.67
  293.1 9.0 all-gather.2
  303.2 7.0 while.65
  310.2 1.9 convolution_bitcast_fusion.1
  312.2 1.9 convolution_add_fusion.2
  314.0 2.0 copy.273
  316.1 2.8 convolution_add_fusion.1
  320.1 2.2 pad_maximum_fusion
  322.3 4.0 fusion.31
  326.5 2.0 fusion.29
  328.7 2.1 fusion.26
  334.0 2.1 fusion.97
  336.1 24.6 %all-reduce.18.cloned.1.call-done = f32[1024,256]{0,1:T(8,128)} async-done(((f32[1024,256]{0,1:T(8,128)}), f32[1024,256]{0,1:T(8,128)}) %all-reduce.18.cloned.1.call-update) | async-done | bytes 1048592 | tf_op jit(solution)/shard_map/psum | solution.py:234
  360.7 5.1 multiply_reduce_fusion.5
  368.6 2.3 pad_add_fusion
  371.0 9.4 collective-permute-done.1
  387.0 30.2 %reduce-window.16 = f32[4,6,2,128]{3,2,1,0:T(2,128)S(1)} reduce-window(f32[4,6,2,128]{3,2,1,0:T(2,128)S(1)} %reshape.220, f32[]{:T(128)} %constant.139.clone.1), window={size=1x1x1x128 pad=0_0x0_0x0_0x0_127}, to_apply=%region_26.27 | reduce-window | flops 780288 | bytes 49156 | tf_op jit(solution)/shard_map/reduce-window.2
  417.4 2.0 fusion.40
  422.9 2.8 fusion.89
  425.7 2.8 add_add_fusion
  431.1 179.3 %reduce-scatter.18.cloned.1.call-done = f32[384,24]{0,1:T(8,128)} async-done(((f32[384,768]{0,1:T(8,128)}), f32[384,24]{0,1:T(8,128)}) %reduce-scatter.18.cloned.1.call-update) | async-done | bytes 36880
  610.4 6.3 all_gather.73
  616.8 219.0 %reduce-scatter.14.cloned.1.call-done = f32[24,384]{1,0:T(8,128)} async-done(((f32[768,384]{1,0:T(8,128)}), f32[24,384]{1,0:T(8,128)}) %reduce-scatter.14.cloned.1.call-update) | async-done | bytes 36880
  835.7 6.3 all_gather.69
  842.1 216.4 %reduce-scatter.12.cloned.1.call-done = f32[24,256]{1,0:T(8,128)} async-done(((f32[768,256]{1,0:T(8,128)}), f32[24,256]{1,0:T(8,128)}) %reduce-scatter.12.cloned.1.call-update) | async-done | bytes 24592 | tf_op jit(solution)/shard_map/reduce_scatter | solution.py:277
  1058.5 6.2 all_gather.72
  1064.7 219.8 %reduce-scatter.16.cloned.1.call-done = f32[24,384]{1,0:T(8,128)} async-done(((f32[768,384]{1,0:T(8,128)}), f32[24,384]{1,0:T(8,128)}) %reduce-scatter.16.cloned.1.call-update) | async-done | bytes 36880
  1284.5 6.5 all_gather.70
  1291.1 5.5 fusion.16
  1296.6 179.8 %all-reduce.13 = (f32[768]{0:T(1024)S(1)}, f32[768,6]{0,1:T(8,128)S(1)}, f32[4,384]{1,0:T(4,128)}, f32[384]{0:T(512)}, f32[4,256]{1,0:T(4,128)}, /*index=5*/f32[...) all-reduce(f32[768]{0:T(1024)S(1)} %get-tuple-element.330, ...), channel_id=5, replica_groups=mesh['dp'=16,'ctx'=2,'tp'=4] {'dp','ctx'}, use_global_device_ids=true, to_apply=%region_31.32.clone | all-reduce | flops 8978 | bytes 71824
  1476.5 5.8 all-gather.4
  1483.2 6.9 all-reduce.7
  1490.1 5.3 fusion.13
  (330 shorter events, 67.0 us)
Async XLA Ops:
  8.0 47.4 %copy-start.56 = (bf16[48,384]{1,0:T(8,128)(2,1)S(1)}, bf16[48,384]{1,0:T(8,128)(2,1)}, u32[]{:S(2)}) copy-start(bf16[48,384]{1,0:T(8,128)(2,1)} %param.27) | copy-start | bytes 110596
  8.0 68.5 %copy-start.66 = (bf16[48,256]{1,0:T(8,128)(2,1)S(1)}, bf16[48,256]{1,0:T(8,128)(2,1)}, u32[]{:S(2)}) copy-start(bf16[48,256]{1,0:T(8,128)(2,1)} %param.29) | copy-start | bytes 73732
  8.0 352.7 %all-reduce.18.cloned.1.call-start = ((), (), s32[]{:S(2)}) async-start(), calls=%async_computation.4 | async-start | bytes 2097152 | tf_op jit(solution)/shard_map/psum | solution.py:234
  52.9 47.7 %copy-start.5 = (bf16[1,1024,768]{2,1,0:T(8,128)(2,1)S(1)}, bf16[1,1024,768]{2,1,0:T(8,128)(2,1)}, u32[]{:S(2)}) copy-start(bf16[1,1024,768]{2,1,0:T(8,128)(2,1)} %param.24) | copy-start | bytes 4718596
  52.9 48.1 %copy-start.46 = (f32[768]{0:T(1024)}, f32[768]{0:T(1024)S(1)}, u32[]{:S(2)}) copy-start(f32[768]{0:T(1024)S(1)} %convert_element_type.92) | copy-start | bytes 9220
  76.5 24.6 %copy-start.34 = (bf16[768,384]{1,0:T(8,128)(2,1)}, bf16[768,384]{1,0:T(8,128)(2,1)S(1)}, u32[]{:S(2)}) copy-start(bf16[768,384]{1,0:T(8,128)(2,1)S(1)} %all_gather.57) | copy-start | bytes 1769476
  101.1 28.5 %copy-start = (bf16[1024,768]{1,0:T(8,128)(2,1)}, bf16[1024,768]{1,0:T(8,128)(2,1)S(1)}, u32[]{:S(2)}) copy-start(bf16[1024,768]{1,0:T(8,128)(2,1)S(1)} %fusion.8) | copy-start | bytes 4718596
  101.9 6.6 copy-start.73
  101.9 27.1 %copy-start.82 = (f32[6]{0:T(128)S(1)}, f32[6]{0:T(128)}, u32[]{:S(2)}) copy-start(f32[6]{0:T(128)} %param.36) | copy-start | bytes 76
  102.0 27.6 %copy-start.78 = (f32[6]{0:T(128)S(1)}, f32[6]{0:T(128)}, u32[]{:S(2)}) copy-start(f32[6]{0:T(128)} %param.35) | copy-start | bytes 76
  102.6 28.1 %copy-start.21 = (bf16[1024,256]{0,1:T(8,128)(2,1)}, bf16[1024,256]{0,1:T(8,128)(2,1)S(1)}, u32[]{:S(2)}) copy-start(bf16[1024,256]{0,1:T(8,128)(2,1)S(1)} %convolution_convert_fusion.1) | copy-start | bytes 1572868
  102.6 36.1 %copy-start.70 = (f32[4,384]{1,0:T(4,128)S(1)}, f32[4,384]{1,0:T(4,128)}, u32[]{:S(2)}) copy-start(f32[4,384]{1,0:T(4,128)} %param.31) | copy-start | bytes 18436
  102.8 35.9 %copy-start.71 = (f32[4,256]{1,0:T(4,128)S(1)}, f32[4,256]{1,0:T(4,128)}, u32[]{:S(2)}) copy-start(f32[4,256]{1,0:T(4,128)} %param.33) | copy-start | bytes 12292
  102.8 36.0 %copy-start.85 = (u32[128]{0:T(128)S(1)}, u32[128]{0:T(128)}, u32[]{:S(2)}) copy-start(u32[128]{0:T(128)} %constant.173) | copy-start | bytes 1540
  102.8 45.2 %copy-start.57 = (bf16[48,384]{1,0:T(8,128)(2,1)S(1)}, bf16[48,384]{1,0:T(8,128)(2,1)}, u32[]{:S(2)}) copy-start(bf16[48,384]{1,0:T(8,128)(2,1)} %param.26) | copy-start | bytes 110596
  102.8 95.7 %collective-permute-start = (bf16[3,640]{0,1:T(8,128)(2,1)S(1)}, bf16[3,640]{0,1:T(8,128)(2,1)}, u32[]{:S(2)}, u32[]{:S(2)}) collective-permute-start(bf16[3,640]{0,1:T(8,128)(2,1)S(1)} %pad_maximum_fusion.1), channel_id=1, source_target_pairs={{0,4},{1,5},{2,6},{3,7},{8,12},{9,13},{10,14},{11,15},{16,20},{17,... | collective-permute-start | bytes 11528 | tf_op jit(solution)/shard_map/ppermute | solution.py:21
  108.5 65.6 %copy-start.58 = (bf16[384,48]{0,1:T(8,128)(2,1)S(1)}, bf16[384,48]{0,1:T(8,128)(2,1)}, u32[]{:S(2)}) copy-start(bf16[384,48]{0,1:T(8,128)(2,1)} %param.30) | copy-start | bytes 110596
  129.6 68.9 %copy-start.74 = (f32[384]{0:T(512)S(1)}, f32[384]{0:T(512)}, u32[]{:S(2)}) copy-start(f32[384]{0:T(512)} %param.32) | copy-start | bytes 4612
  129.6 68.9 %copy-start.77 = (f32[256]{0:T(256)S(1)}, f32[256]{0:T(256)}, u32[]{:S(2)}) copy-start(f32[256]{0:T(256)} %param.34) | copy-start | bytes 3076
  138.8 61.7 %copy-start.48 = (f32[640]{0:T(1024)}, f32[640]{0:T(1024)S(1)}, u32[]{:S(2)}) copy-start(f32[640]{0:T(1024)S(1)} %get-tuple-element.335) | copy-start | bytes 7684
  138.8 61.7 %copy-start.50 = (f32[640]{0:T(1024)}, f32[640]{0:T(1024)S(1)}, u32[]{:S(2)}) copy-start(f32[640]{0:T(1024)S(1)} %get-tuple-element.336) | copy-start | bytes 7684
  138.8 61.7 %copy-start.52 = (f32[640]{0:T(1024)}, f32[640]{0:T(1024)S(1)}, u32[]{:S(2)}) copy-start(f32[640]{0:T(1024)S(1)} %get-tuple-element.337) | copy-start | bytes 7684
  138.8 61.7 %copy-start.54 = (f32[640]{0:T(1024)}, f32[640]{0:T(1024)S(1)}, u32[]{:S(2)}) copy-start(f32[640]{0:T(1024)S(1)} %get-tuple-element.338) | copy-start | bytes 7684
  198.4 111.8 %copy-start.41 = (f32[4,256,6]{1,2,0:T(8,128)}, f32[4,256,6]{1,2,0:T(8,128)S(1)}, u32[]{:S(2)}) copy-start(f32[4,256,6]{1,2,0:T(8,128)S(1)} %get-tuple-element.410) | copy-start | bytes 73732
  198.5 89.1 %copy-start.39 = (f32[4,256,6]{1,2,0:T(8,128)}, f32[4,256,6]{1,2,0:T(8,128)S(1)}, u32[]{:S(2)}) copy-start(f32[4,256,6]{1,2,0:T(8,128)S(1)} %copy.222) | copy-start | bytes 73732
  237.5 5.5 copy-start.75
  244.8 2.4 copy-start.14
  248.6 4.5 copy-start.16
  250.4 8.7 copy-start.64
  278.1 2.6 copy-start.11
  278.1 2.6 copy-start.12
  280.7 6.9 copy-start.7
  288.9 13.2 copy-start.72
  312.2 3.9 copy-start.31
  322.3 4.2 copy-start.38
  322.3 288.1 %reduce-scatter.18.cloned.1.call-start = ((), (), s32[]{:S(2)}) async-start(), calls=%async_computation.8 | async-start | bytes 1216512
  326.4 2.2 copy-start.42
  326.4 2.2 copy-start.45
  326.4 2.2 copy-start.62
  326.4 2.2 copy-start.81
  326.5 509.3 %reduce-scatter.14.cloned.1.call-start = ((), (), s32[]{:S(2)}) async-start(), calls=%async_computation.6 | async-start | bytes 1216512
  326.5 2.1 copy-start.37
  331.8 2.2 copy-start.25
  336.0 722.4 %reduce-scatter.12.cloned.1.call-start = ((), (), s32[]{:S(2)}) async-start(), calls=%async_computation.5 | async-start | bytes 811008 | tf_op jit(solution)/shard_map/reduce_scatter | solution.py:277
  360.7 5.2 copy-start.49
  360.7 5.2 copy-start.51
  360.7 5.2 copy-start.53
  360.7 5.2 copy-start.55
  366.9 13.4 collective-permute-start.1
  371.0 11.1 copy-start.3
  383.6 900.9 %reduce-scatter.16.cloned.1.call-start = ((), (), s32[]{:S(2)}) async-start(), calls=%async_computation.7 | async-start | bytes 1216512
  385.3 32.0 %copy-start.19 = (bf16[1024,640]{0,1:T(8,128)(2,1)S(1)}, bf16[1024,640]{0,1:T(8,128)(2,1)}, u32[]{:S(2)}) copy-start(bf16[1024,640]{0,1:T(8,128)(2,1)} %copy-done.18) | copy-start | bytes 3932164
  417.4 2.4 copy-start.63
  417.4 2.4 copy-start.79
  417.4 2.5 copy-start.43
  419.5 871.6 %all-reduce.20.cloned.1.call-start = ((), (), s32[]{:S(2)}) async-start(), calls=%async_computation.9 | async-start | bytes 12582912 | tf_op jit(solution)/shard_map/psum | solution.py:160
  422.9 2.8 copy-start.20
  422.9 2.8 copy-start.35
  428.5 2.2 copy-start.83
  428.5 862.5 %copy-start.24 = (bf16[768,256]{1,0:T(8,128)(2,1)S(1)}, bf16[768,256]{1,0:T(8,128)(2,1)}, u32[]{:S(2)}) copy-start(bf16[768,256]{1,0:T(8,128)(2,1)} %copy-done.23) | copy-start | bytes 1179652
  428.5 862.5 %copy-start.47 = (f32[768]{0:T(1024)S(1)}, f32[768]{0:T(1024)}, u32[]{:S(2)}) copy-start(f32[768]{0:T(1024)} %copy-done.46) | copy-start | bytes 9220
  1291.1 5.5 copy-start.68
  1291.1 199.0 %copy-start.6 = (bf16[1,1024,768]{2,1,0:T(8,128)(2,1)S(1)}, bf16[1,1024,768]{2,1,0:T(8,128)(2,1)}, u32[]{:S(2)}) copy-start(bf16[1,1024,768]{2,1,0:T(8,128)(2,1)} %param.24) | copy-start | bytes 4718596
  1291.1 199.0 %copy-start.67 = (f32[1024]{0:T(1024)S(1)}, f32[1024]{0:T(1024)}, u32[]{:S(2)}) copy-start(f32[1024]{0:T(1024)} %get-tuple-element.411) | copy-start | bytes 12292
  (30 other events, 49.3 us)
Sparse Core Ops, SparseCore 0:
  322.4 38.2 all-reduce.17
  428.6 125.7 all-reduce.19
Sparse Core Ops, SparseCore 1:
  328.3 282.1 reduce-scatter.17
  615.1 220.5 reduce-scatter.13
  841.1 217.3 reduce-scatter.11
  1063.9 220.6 reduce-scatter.15
where the time goes:
time: 1520 us; the launch traced here: 1510 us
  waiting for transfers between devices  869 us (57%)
  blocking collectives  410 us (27%)
  other arithmetic  91.6 us (6%)
  matrix products  60.6 us (4%)
  local copies, waits for them, and re-layouts  46.6 us (3%)
  between operations  19.8 us (1%)
    unnamed x9, waiting for transfers between devices  618 us
    unnamed x4, blocking collectives  235 us
    reduce_scatter x1, waiting for transfers between devices, per_device(): lax.psum_scatter(grad_w_state, ('dp', 'ctx'), scatter_dimension=0, tiled=...  216 us
    another operation x8, other arithmetic  42.7 us
  transfers between devices with their start and end apart: 8, of which 6 were waited for; matrix products, arithmetic and copies ran while one was open for 5% of the time, Pallas kernels for 0%

commit v1 on v0

v1 whole, which is shorter than its diff:
```python
import jax
import jax.numpy as jnp
from jax import lax
from jax.experimental import pallas as pl
from jax.experimental.pallas import tpu as pltpu
from jax.sharding import PartitionSpec as P

D = 768
HEAD = 64
STATE = 128
CONV = 4
GROUP = 256
INNER = 1536


EPS = 1e-05
HIGH = lax.Precision.HIGHEST


MESH = pl.DeviceIdType.MESH
VM = pl.BlockSpec(memory_space=pltpu.VMEM)
ANY = pl.BlockSpec(memory_space=pl.ANY)
DP = 16
ROWS = 48
WIDE = 1536
DMA = pltpu.SemaphoreType.DMA


def params(ident, limit=32):
    return pltpu.CompilerParams(
        collective_id=ident, has_side_effects=True, vmem_limit_bytes=limit * 1024 * 1024
    )


def remote(source, target, send, recv, **where):
    return pltpu.make_async_remote_copy(
        src_ref=source,
        dst_ref=target,
        send_sem=send,
        recv_sem=recv,
        device_id=where,
        device_id_type=MESH,
    )


def greet(peers):
    barrier = pltpu.get_barrier_semaphore()
    for where in peers:
        pl.semaphore_signal(barrier, inc=1, device_id=where, device_id_type=MESH)
    pl.semaphore_wait(barrier, len(peers))


def dp_ring():
    me = lax.axis_index("dp")
    return me, [lax.rem(me + hop, DP) for hop in range(1, DP)]


def gather_kernel(shard, edge, full, edge_in, send, recv, edge_send, edge_recv, own):
    me, others = dp_ring()
    partner = 1 - lax.axis_index("ctx")
    greet([{"dp": peer} for peer in others] + [{"ctx": partner}])
    mine = pl.ds(pl.multiple_of(me * ROWS, 16), ROWS)
    copies = [remote(edge, edge_in, edge_send, edge_recv, ctx=partner)]
    copies += [
        remote(shard, full.at[mine], send.at[hop], recv.at[hop], dp=peer)
        for hop, peer in enumerate(others)
    ]
    for copy in copies:
        copy.start()
    keep = pltpu.make_async_copy(shard, full.at[mine], own)
    keep.start()
    keep.wait()
    for copy in copies:
        copy.wait()


def gather_weights(shard, edge):
    return pl.pallas_call(
        gather_kernel,
        out_shape=(
            jax.ShapeDtypeStruct((DP * ROWS, WIDE), shard.dtype),
            jax.ShapeDtypeStruct(edge.shape, edge.dtype),
        ),
        in_specs=[VM, VM],
        out_specs=(VM, VM),
        scratch_shapes=[DMA((DP - 1,)), DMA((DP - 1,)), DMA, DMA, DMA],
        compiler_params=params(1),
    )(shard, edge)


def scatter_kernel(
    grads, small, out, small_out, held, small_held, total, arrived, total_in, arrived_in,
    send, recv, small_send, small_recv, pair_send, pair_recv, own
):
    me, others = dp_ring()
    partner = 1 - lax.axis_index("ctx")
    greet([{"dp": peer} for peer in others] + [{"ctx": partner}])
    copies = []
    for hop, peer in enumerate(others):
        rows = pl.ds(pl.multiple_of(peer * ROWS, 16), ROWS)
        copies.append(remote(grads.at[rows], held.at[me], send.at[hop], recv.at[hop], dp=peer))
        copies.append(
            remote(small, small_held.at[me], small_send.at[hop], small_recv.at[hop], dp=peer)
        )
    for copy in copies:
        copy.start()
    rows = pl.ds(pl.multiple_of(me * ROWS, 16), ROWS)
    keeps = [
        pltpu.make_async_copy(grads.at[rows], held.at[me], own.at[0]),
        pltpu.make_async_copy(small, small_held.at[me], own.at[1]),
    ]
    for keep in keeps:
        keep.start()
    for keep in keeps:
        keep.wait()
    for copy in copies:
        copy.wait()
    total[...] = jnp.zeros_like(total)
    arrived[...] = jnp.zeros_like(arrived)

    def add(index, carry):
        total[...] += held[index].astype(jnp.float32)
        arrived[...] += small_held[index]
        return carry

    lax.fori_loop(0, DP, add, 0)
    pairs = [
        remote(total, total_in, pair_send.at[0], pair_recv.at[0], ctx=partner),
        remote(arrived, arrived_in, pair_send.at[1], pair_recv.at[1], ctx=partner),
    ]
    for copy in pairs:
        copy.start()
    for copy in pairs:
        copy.wait()
    out[...] = total[...] + total_in[...]
    small_out[...] = arrived[...] + arrived_in[...]


def scatter_grads(grads, small):
    block = (ROWS, WIDE)
    f32 = jnp.float32
    return pl.pallas_call(
        scatter_kernel,
        out_shape=(
            jax.ShapeDtypeStruct(block, f32),
            jax.ShapeDtypeStruct(small.shape, f32),
        ),
        in_specs=[VM, VM],
        out_specs=(VM, VM),
        scratch_shapes=[
            pltpu.VMEM((DP, *block), grads.dtype),
            pltpu.VMEM((DP, *small.shape), f32),
            pltpu.VMEM(block, f32),
            pltpu.VMEM(small.shape, f32),
            pltpu.VMEM(block, f32),
            pltpu.VMEM(small.shape, f32),
            DMA((DP - 1,)),
            DMA((DP - 1,)),
            DMA((DP - 1,)),
            DMA((DP - 1,)),
            DMA((2,)),
            DMA((2,)),
            DMA((2,)),
        ],
        compiler_params=params(2),
    )(grads, small)


def swap_kernel(mine, other, send, recv):
    partner = 1 - lax.axis_index("ctx")
    greet([{"ctx": partner}])
    copy = remote(mine, other, send, recv, ctx=partner)
    copy.start()
    copy.wait()


def swap_ctx(value, ident):
    return pl.pallas_call(
        swap_kernel,
        out_shape=jax.ShapeDtypeStruct(value.shape, value.dtype),
        in_specs=[VM],
        out_specs=VM,
        scratch_shapes=[DMA, DMA],
        compiler_params=params(ident),
    )(value)


def sum_all_kernel(part, out, held, send, recv):
    me = lax.axis_index("tp")
    others = [lax.rem(me + hop, 4) for hop in range(1, 4)]
    greet([{"tp": peer} for peer in others])
    copies = [
        remote(part, held.at[me], send.at[hop], recv.at[hop], tp=peer)
        for hop, peer in enumerate(others)
    ]
    for copy in copies:
        copy.start()
    held[me] = part[...]
    for copy in copies:
        copy.wait()
    out[...] = (held[0] + held[1]) + (held[2] + held[3])


def sum_all(part, ident):
    return pl.pallas_call(
        sum_all_kernel,
        out_shape=jax.ShapeDtypeStruct(part.shape, part.dtype),
        in_specs=[VM],
        out_specs=VM,
        scratch_shapes=[pltpu.VMEM((4, *part.shape), part.dtype), DMA((3,)), DMA((3,))],
        compiler_params=params(ident),
    )(part)


def tp_sum_kernel(part, base, out, half_in, quarter_out, quarter_in, send, recv):
    me = lax.axis_index("tp")
    core, chip = lax.rem(me, 2), lax.div(me, 2)
    twin, across = me + 1 - 2 * core, me + 2 - 4 * chip
    greet([{"tp": twin}, {"tp": across}])
    size = part.shape[0] // 4

    def quarter(c, h):
        return pl.ds(pl.multiple_of((2 * c + h) * size, size), size)

    keep, give = quarter(core, chip), quarter(core, 1 - chip)
    for_twin = [quarter(1 - core, 1 - chip), quarter(1 - core, chip)]
    first = [
        remote(part.at[rows], half_in.at[place], send.at[place], recv.at[place], tp=twin)
        for place, rows in enumerate(for_twin)
    ]
    for copy in first:
        copy.start()
    f32 = jnp.float32
    first[0].wait()
    quarter_out[...] = (part[give].astype(f32) + half_in[0].astype(f32)).astype(part.dtype)
    over = remote(quarter_out, quarter_in, send.at[2], recv.at[2], tp=across)
    over.start()
    first[1].wait()
    over.wait()
    total = part[keep].astype(f32) + half_in[1].astype(f32) + quarter_in[...].astype(f32)
    if base is not None:
        total = total + base[keep].astype(f32)
    out[keep] = total.astype(out.dtype)
    back = remote(out.at[keep], out.at[keep], send.at[3], recv.at[3], tp=across)
    beside = remote(out.at[keep], out.at[keep], send.at[4], recv.at[4], tp=twin)
    back.start()
    beside.start()
    back.wait()
    relay = remote(out.at[give], out.at[give], send.at[5], recv.at[5], tp=twin)
    relay.start()
    beside.wait()
    relay.wait()


def tp_sum_bare(part, out, *rest):
    tp_sum_kernel(part, None, out, *rest)


def tp_sum(part, base, ident):
    rows, columns = part.shape
    operands = (part,) if base is None else (part, base)
    return pl.pallas_call(
        tp_sum_bare if base is None else tp_sum_kernel,
        out_shape=jax.ShapeDtypeStruct(part.shape, part.dtype),
        in_specs=[VM] * len(operands),
        out_specs=VM,
        scratch_shapes=[
            pltpu.VMEM((2, rows // 4, columns), part.dtype),
            pltpu.VMEM((rows // 4, columns), part.dtype),
            pltpu.VMEM((rows // 4, columns), part.dtype),
            DMA((6,)),
            DMA((6,)),
        ],
        compiler_params=params(ident),
    )(*operands)


def matmul(left, right):
    return jnp.dot(left, right, preferred_element_type=jnp.float32)


def back_matmul(grad_rows, weight):
    return lax.dot_general(
        grad_rows, weight, (((1,), (1,)), ((), ())), preferred_element_type=jnp.float32
    )


def silu_grad(pre_act):
    sigmoid_val = jax.nn.sigmoid(pre_act)
    return sigmoid_val * (1.0 + pre_act * (1.0 - sigmoid_val))


def chain(entering, decay, fresh, order):
    carry, inputs = entering, {}
    for block in order:
        inputs[block] = carry
        carry = decay[block][:, None, None] * carry + fresh[block]
    return carry, jnp.stack([inputs[block] for block in sorted(inputs)])


def per_device(
    stream,
    norm_gain,
    w_gate,
    w_value,
    w_step,
    w_state,
    w_out,
    conv_value,
    conv_value_bias,
    conv_state,
    conv_state_bias,
    step_bias,
    decay_log,
    skip_gain,
    inner_gain,
    cotangent,
):
    tokens = stream.shape[1]
    local_heads = step_bias.shape[0]
    local_inner = inner_gain.shape[0]
    blocks = tokens // GROUP
    bfloat = jnp.bfloat16
    f32 = jnp.float32
    ctx = lax.axis_index("ctx")
    tp = lax.axis_index("tp")
    mix = local_inner + 2 * STATE
    thin = mix + local_inner
    shard = jnp.concatenate(
        [
            w_value,
            w_state,
            w_gate,
            w_step,
            norm_gain[:, None],
            jnp.zeros((ROWS, 128 - local_heads - 1), bfloat),
            w_out.T,
        ],
        axis=1,
    )
    full, edge = gather_weights(shard, stream[0, tokens - 16 :])
    projection = full[:, : thin + 128]
    out_t = full[:, thin + 128 :]
    gain_zero = full[:, thin + local_heads].astype(f32)[None]
    source = stream[0].astype(f32)

    def normalise(rows):
        scale = lax.rsqrt(jnp.mean(rows * rows, axis=-1, keepdims=True) + EPS)
        return scale, (rows * scale * gain_zero).astype(bfloat)

    scale_zero, normed = normalise(source)
    projected = matmul(normed, projection)
    conv_input = projected[:, :mix].astype(bfloat)
    gate_out = projected[:, mix:thin]
    step_raw = projected[:, thin : thin + local_heads]
    edge_normed = normalise(edge.astype(f32))[1]
    edge_rows = matmul(edge_normed, full[:, :mix])[13:]
    edge_rows = jnp.where(ctx == 0, 0.0, edge_rows).astype(bfloat)
    padded = jnp.concatenate([edge_rows, conv_input], axis=0).astype(f32)
    kernel = jnp.concatenate([conv_value, conv_state], axis=1)
    kernel_bias = jnp.concatenate([conv_value_bias, conv_state_bias])
    conv_sum = kernel_bias + sum(
        (kernel[offset] * padded[offset : offset + tokens] for offset in range(CONV))
    )
    activated = jax.nn.silu(conv_sum)
    values = activated[:, :local_inner].astype(bfloat).reshape(blocks, GROUP, local_heads, HEAD)
    keys_low = (
        activated[:, local_inner : local_inner + STATE].astype(bfloat).reshape(blocks, GROUP, STATE)
    )
    reads_low = activated[:, local_inner + STATE :].astype(bfloat).reshape(blocks, GROUP, STATE)
    step_val = jax.nn.softplus(step_raw + step_bias)
    decay_rate = jnp.exp(decay_log)
    log_rate = -decay_rate * step_val
    step_blocks = step_val.reshape(blocks, GROUP, local_heads).transpose(0, 2, 1)
    lower_mask = jnp.arange(GROUP)[:, None] >= jnp.arange(GROUP)[None, :]
    lower_ones = lower_mask.astype(f32)
    cum_log = jnp.einsum(
        "ts,csh->cht", lower_ones, log_rate.reshape(blocks, GROUP, local_heads), precision=HIGH
    )
    last_cum = cum_log[:, :, -1]
    decays = jnp.exp(jnp.where(lower_mask, cum_log[:, :, :, None] - cum_log[:, :, None, :], -1e30))
    inner_prod = jnp.einsum("ctn,csn->cts", reads_low, keys_low, preferred_element_type=f32)
    weights = inner_prod[:, None] * decays * step_blocks[:, :, None, :]
    weights_low = weights.astype(bfloat)
    local_out = jnp.einsum("chts,cshp->cthp", weights_low, values, preferred_element_type=f32)
    scales = step_blocks * jnp.exp(last_cum[:, :, None] - cum_log)
    scales_t = scales.transpose(0, 2, 1)
    values_f = values.astype(f32)
    weighted = (values_f * scales_t[..., None]).astype(bfloat)
    fresh_state = jnp.einsum("cshp,csn->chpn", weighted, keys_low, preferred_element_type=f32)
    block_decay = jnp.exp(last_cum)
    zero_state = jnp.zeros((local_heads, HEAD, STATE), f32)
    forward, backward = range(blocks), range(blocks - 1, -1, -1)
    device_state = chain(zero_state, block_decay, fresh_state, forward)[0]
    entering = jnp.where(ctx == 1, swap_ctx(device_state, 3), 0.0)
    states_in = chain(entering, block_decay, fresh_state, forward)[1]
    states_low = states_in.astype(bfloat)
    carried_pre = jnp.einsum("ctn,chpn->cthp", reads_low, states_low, preferred_element_type=f32)
    exp_cum = jnp.exp(cum_log).transpose(0, 2, 1)
    ssd_heads = (
        local_out + exp_cum[..., None] * carried_pre + skip_gain[None, None, :, None] * values_f
    )
    ssd_out = ssd_heads.reshape(tokens, local_inner)
    gate_act = jax.nn.silu(gate_out)
    gated = ssd_out * gate_act
    upstream = cotangent[0]
    grad_normal = matmul(upstream, out_t)
    scaled_grad = grad_normal * inner_gain
    sums = jnp.stack([jnp.sum(gated * gated, axis=1), jnp.sum(scaled_grad * gated, axis=1)])
    sums = sum_all(sums.reshape(2 * tokens // 128, 128), 4).reshape(2, tokens)
    square_sum, cross_sum = sums[0], sums[1]
    scale_one = lax.rsqrt(square_sum / INNER + EPS)[:, None]
    normal_out = (gated * scale_one * inner_gain).astype(bfloat)
    branch = back_matmul(normal_out, out_t).astype(bfloat)
    mixed_out = tp_sum(branch, stream[0], 5)[None]
    grad_w_out = matmul(upstream.T, normal_out)
    grad_inner_gain = jnp.sum(grad_normal * gated * scale_one, axis=0)
    grad_gated = (
        scale_one * scaled_grad
        - gated * (scale_one * scale_one * scale_one) * (cross_sum / INNER)[:, None]
    )
    grad_ssd = (grad_gated * gate_act).astype(bfloat)
    grad_gate = (grad_gated * ssd_out * silu_grad(gate_out)).astype(bfloat)
    grad_heads = grad_ssd.reshape(blocks, GROUP, local_heads, HEAD)
    grad_heads_f = grad_heads.astype(f32)
    grad_skip_gain = jnp.sum(grad_heads_f * values_f, axis=(0, 1, 3))
    grad_values = skip_gain[None, None, :, None] * grad_heads_f
    grad_weights = jnp.einsum("cthp,cshp->chts", grad_heads, values, preferred_element_type=f32)
    grad_values = grad_values + jnp.einsum(
        "chts,cthp->cshp", weights_low, grad_heads, preferred_element_type=f32
    )
    product = grad_weights * weights
    grad_cum = jnp.sum(product, axis=3) - jnp.sum(product, axis=2)
    grad_step = jnp.sum(grad_weights * inner_prod[:, None] * decays, axis=2)
    grad_inner = jnp.sum(grad_weights * decays * step_blocks[:, :, None, :], axis=1)
    grad_exp = grad_heads_f * exp_cum[..., None]
    grad_carried = grad_exp.astype(bfloat)
    grad_cum = grad_cum + jnp.sum(grad_exp * carried_pre, axis=3).transpose(0, 2, 1)
    grad_reads = jnp.einsum("cthp,chpn->ctn", grad_carried, states_low, preferred_element_type=f32)
    grad_state_read = jnp.einsum(
        "cthp,ctn->chpn", grad_carried, reads_low, preferred_element_type=f32
    )
    local_in = chain(zero_state, block_decay, grad_state_read, backward)[0]
    arriving = jnp.where(ctx == 0, swap_ctx(local_in, 6), 0.0)
    grad_state_out = chain(arriving, block_decay, grad_state_read, backward)[1]
    grad_last = jnp.sum(grad_state_out * states_in, axis=(2, 3)) * block_decay
    grad_fresh = grad_state_out.astype(bfloat)
    grad_weighted = jnp.einsum("csn,chpn->cshp", keys_low, grad_fresh, preferred_element_type=f32)
    grad_keys = jnp.einsum("cshp,chpn->csn", weighted, grad_fresh, preferred_element_type=f32)
    grad_values = grad_values + grad_weighted * scales_t[..., None]
    grad_scales = jnp.sum(grad_weighted * values_f, axis=3).transpose(0, 2, 1)
    grad_step = grad_step + grad_scales * jnp.exp(last_cum[:, :, None] - cum_log)
    spill_term = grad_scales * scales
    grad_last = grad_last + jnp.sum(spill_term, axis=2)
    last_flag = (jnp.arange(GROUP) == GROUP - 1).astype(f32)
    grad_cum = grad_cum - spill_term + grad_last[:, :, None] * last_flag
    keys_f = keys_low.astype(f32)
    reads_f = reads_low.astype(f32)
    grad_reads = grad_reads + jnp.einsum("cts,csn->ctn", grad_inner, keys_f, precision=HIGH)
    grad_keys = grad_keys + jnp.einsum("cts,ctn->csn", grad_inner, reads_f, precision=HIGH)
    grad_rate = jnp.einsum("ts,cht->chs", lower_ones, grad_cum, precision=HIGH)
    grad_step = grad_step - decay_rate[None, :, None] * grad_rate
    grad_decay_log = -decay_rate * jnp.sum(grad_rate * step_blocks, axis=(0, 2))
    grad_step_pre = grad_step.transpose(0, 2, 1).reshape(tokens, local_heads) * jax.nn.sigmoid(
        step_raw + step_bias
    )
    grad_step_bias = jnp.sum(grad_step_pre, axis=0)
    grad_step_low = grad_step_pre.astype(bfloat)
    state_grads = jnp.concatenate(
        [grad_keys.reshape(tokens, STATE), grad_reads.reshape(tokens, STATE)], axis=1
    )
    state_grads = sum_all(state_grads, 7)
    grad_act = jnp.concatenate([grad_values.reshape(tokens, local_inner), state_grads], axis=1)
    grad_conv = grad_act * silu_grad(conv_sum)
    grad_padded = sum(
        (
            jnp.pad(kernel[offset] * grad_conv, ((offset, CONV - 1 - offset), (0, 0)))
            for offset in range(CONV)
        )
    )
    incoming = swap_ctx(grad_padded[:8], 8)[: CONV - 1]
    incoming = jnp.where(ctx == 0, incoming, 0.0)
    grad_input = grad_padded[CONV - 1 :] + jnp.pad(incoming, ((tokens - (CONV - 1), 0), (0, 0)))
    grad_kernel = jnp.stack(
        [jnp.sum(grad_conv * padded[offset : offset + tokens], axis=0) for offset in range(CONV)]
    )
    grad_kernel_bias = jnp.sum(grad_conv, axis=0)
    grad_step_wide = jnp.pad(grad_step_low, ((0, 0), (0, 128 - local_heads)))
    grad_mix = grad_input.astype(bfloat)
    all_grads = jnp.concatenate([grad_mix, grad_gate, grad_step_wide], axis=1)
    grad_w = matmul(normed.T, all_grads)
    mine = (jnp.arange(tokens) // (tokens // 4) == tp)[:, None]
    state_mine = jnp.where(mine, grad_mix[:, local_inner:], 0)
    once = jnp.concatenate([grad_mix[:, :local_inner], state_mine, all_grads[:, mix:]], axis=1)
    grad_normed = tp_sum(back_matmul(once, projection).astype(bfloat), None, 9).astype(f32)
    grad_norm_gain = jnp.sum(grad_normed * source * scale_zero, axis=0)
    scaled_zero = grad_normed * gain_zero
    grad_source = scale_zero * scaled_zero - source * (scale_zero * scale_zero * scale_zero) * (
        jnp.sum(scaled_zero * source, axis=1, keepdims=True) / D
    )
    d_stream = (upstream.astype(f32) + grad_source)[None]
    packed = jnp.concatenate(
        [
            grad_w[:, : thin + local_heads],
            grad_norm_gain[:, None],
            grad_w[:, thin + local_heads + 1 :],
            grad_w_out,
        ],
        axis=1,
    ).astype(bfloat)
    heads_row = jnp.concatenate([grad_step_bias, grad_decay_log, grad_skip_gain])
    small = jnp.concatenate(
        [
            grad_kernel[:, :local_inner],
            grad_kernel_bias[None, :local_inner],
            grad_inner_gain[None],
            jnp.pad(grad_kernel[:, local_inner:], ((0, 0), (0, local_inner - 2 * STATE))),
            jnp.pad(grad_kernel_bias[None, local_inner:], ((0, 0), (0, local_inner - 2 * STATE))),
            jnp.pad(heads_row[None], ((0, 4), (0, local_inner - 3 * local_heads))),
        ],
        axis=0,
    )
    owned, totals = scatter_grads(packed, small)
    return (
        mixed_out,
        d_stream,
        owned[:, thin + local_heads],
        owned[:, mix:thin],
        owned[:, :local_inner],
        owned[:, thin : thin + local_heads],
        owned[:, local_inner:mix],
        owned[:, thin + 128 :].T,
        totals[:4, :local_inner],
        totals[4],
        totals[6:10, : 2 * STATE],
        totals[10, : 2 * STATE],
        totals[11, :local_heads],
        totals[11, local_heads : 2 * local_heads],
        totals[11, 2 * local_heads : 3 * local_heads],
        totals[5],
    )


def solution(mesh):
    in_specs = (
        P("dp", "ctx", None),
        P("dp"),
        P("dp", "tp"),
        P("dp", "tp"),
        P("dp", "tp"),
        P("dp", None),
        P("tp", "dp"),
        P(None, "tp"),
        P("tp"),
        P(),
        P(),
        P("tp"),
        P("tp"),
        P("tp"),
        P("tp"),
        P("dp", "ctx", None),
    )
    out_specs = (
        P("dp", "ctx", None),
        P("dp", "ctx", None),
        P("dp"),
        P("dp", "tp"),
        P("dp", "tp"),
        P("dp", "tp"),
        P("dp", None),
        P("tp", "dp"),
        P(None, "tp"),
        P("tp"),
        P(),
        P(),
        P("tp"),
        P("tp"),
        P("tp"),
        P("tp"),
    )
    return jax.shard_map(
        per_device, mesh=mesh, in_specs=in_specs, out_specs=out_specs, check_vma=False
    )
```

time: 1520 us -> 342 us (0.23)
  waiting for transfers between devices: 869 us -> 0 us
  blocking collectives: 410 us -> 0 us
  Pallas kernels: 0 us -> 220 us
  other arithmetic: 91.6 us -> 31.2 us
  matrix products: 60.6 us -> 40.5 us
  between operations: 19.8 us -> 1.9 us
    unnamed x9 -> x0, waiting for transfers between devices: 618 us -> none
    unnamed x4 -> x0, blocking collectives: 235 us -> none
    pallas_call x0 -> x9, Pallas kernels: none -> 220 us  [the longest x1 59.3 us: scatter_grads(): pl.pallas_call(scatter_kernel, out_shape=(jax.ShapeDtypeStruct(block, f32...]
    reduce_scatter x1 -> x0, waiting for transfers between devices: 216 us -> none  [per_device(): lax.psum_scatter(grad_w_state, ('dp', 'ctx'), scatter_dimension=0, tiled=...]
    all_gather x12 -> x0, blocking collectives: 164 us -> none  [the longest x1 26.2 us: per_device(): lax.all_gather(w_gate, 'dp', axis=0, tiled=True)]
    another operation x9 -> x6, other arithmetic: 42.8 us -> 5.52 us
    psum x2 -> x0, waiting for transfers between devices: 24.6 us -> none  [the longest x1 24.6 us: per_device(): state_grads = lax.psum(state_grads, 'tp')]
    add x17 -> x2, other arithmetic: 16.4 us -> 1.09 us  [chain(): carry = decay[block][:, None, None] * carry + fresh[block]]
  transfers between devices with their start and end apart: 8 -> 0, of which waited for: 6 -> 0; matrix products, arithmetic and copies ran while one was open for 5% -> 0% of each run, Pallas kernels for 0% -> 0%
where the time goes in v1:
time: 342 us; the launch traced here: 339 us
  Pallas kernels  220 us (64%)
  local copies, waits for them, and re-layouts  45.2 us (13%)
  matrix products  40.5 us (12%)
  other arithmetic  31.2 us (9%)
    pallas_call x1, Pallas kernels, scatter_grads(): pl.pallas_call(scatter_kernel, out_shape=(jax.ShapeDtypeStruct(block, f32...  59.3 us
    pallas_call x2, Pallas kernels, sum_all(): pl.pallas_call(sum_all_kernel, out_shape=jax.ShapeDtypeStruct(part.shape,...  51 us
    pallas_call x2, Pallas kernels, tp_sum(): pl.pallas_call(tp_sum_bare if base is None else tp_sum_kernel, out_shape=...  48.7 us
    pallas_call x1, Pallas kernels, gather_weights(): pl.pallas_call(gather_kernel, out_shape=(jax.ShapeDtypeStruct((DP * ROWS,...  40.3 us
    pallas_call x3, Pallas kernels, swap_ctx(): pl.pallas_call(swap_kernel, out_shape=jax.ShapeDtypeStruct(value.shape, v...  21.2 us
    dot_general x5, matrix products, matmul(): return jnp.dot(left, right, preferred_element_type=jnp.float32)  13.5 us
    unnamed x141, local copies, waits for them, and re-layouts  13.1 us

profile of v1, /device:TPU:0, one launch (start us, length us, event | category | flops | bytes accessed | tf_op | source)
XLA Modules:
  0.0 339.2 jit_solution(10405433204081526374)
XLA Ops:
  0.7 0.9 copy.104
  1.6 0.8 copy.105
  2.3 0.9 concatenate.38.shard
  3.2 0.7 slice_bitcast_fusion.9.edge
  4.0 40.3 %shard_map.279 = (bf16[768,1536]{1,0:T(8,128)(2,1)S(1)}, bf16[16,768]{1,0:T(8,128)(2,1)S(1)}) custom-call(bf16[48,1536]{1,0:T(8,128)(2,1)S(1)} %concatenate.38.shard, bf16[16,768]{1,0:T(8,128)(2,1)S(1)} %slice_bitcast_fusion.9.edge), custom_call_target="tpu_custom_call" | custom-call | tf_op jit(solution)/shard_map/pallas_call | solution.py:78
  44.5 2.4 fusion.9
  47.6 2.3 fusion.51
  49.9 2.1 copy-done.15
  53.6 1.5 fusion.65
  55.1 1.9 slice.418
  57.8 2.8 multiply_convert_fusion
  60.6 1.0 slice.287
  61.5 2.3 copy.106
  63.9 2.6 reshape.170
  66.5 1.6 fusion.68
  69.2 7.3 %shard_map.280 = f32[6,64,128]{2,1,0:T(8,128)S(1)} custom-call(f32[6,64,128]{2,1,0:T(8,128)S(1)} %fusion.93.mine), custom_call_target="tpu_custom_call" | custom-call | tf_op jit(solution)/shard_map/pallas_call | solution.py:178
  76.5 1.2 fusion.100
  77.7 1.3 add_bitcast_fusion.1
  80.3 2.0 fusion.41
  82.4 1.0 copy.114
  83.4 1.5 copy.139
  84.9 3.1 copy.115
  87.9 5.4 %multiply_reduce_fusion.8 = (f32[1024]{0:T(1024)S(1)}, f32[1024]{0:T(1024)S(1)}, f32[1024,384]{1,0:T(8,128)}, f32[384,1024]{0,1:T(8,128)}) fusion(f32[384]{0:T(512)S(1)} %copy-done.49, f32[1024,384]{1,0:T(8,128)} %copy.115, f32[1024,1152]{1,0:T(8,128)} %copy-done.15, bf16[768,1536]{1,0:T(8,128)(2,1)} %copy-done.2, bf16[1,1024,768]{2,1,0:T(8,128)(2,1)} %param.31), kind=kOutput, calls=%fused_computation.81 | convolution fusion | flops 607909888 | bytes 8463872 | tf_op jit(solution)/shard_map/dot_general | solution.py:279
  93.3 3.7 %shard_map.281 = f32[16,128]{1,0:T(8,128)S(1)} custom-call(f32[16,128]{1,0:T(8,128)S(1)} %reshape.176.part), custom_call_target="tpu_custom_call" | custom-call | tf_op jit(solution)/shard_map/pallas_call | solution.py:205
  97.1 5.1 %multiply_reduce_fusion.6 = (f32[384]{0:T(512)}, bf16[1024,384]{1,0:T(8,128)(2,1)}, bf16[1024,384]{1,0:T(8,128)(2,1)}, f32[384]{0:T(512)}) fusion(bf16[1024,640]{1,0:T(8,128)(2,1)S(1)} %get-tuple-element.121, f32[1024,1152]{1,0:T(8,128)} %copy-done.15, f32[1024]{0:T(1024)S(1)} %get-tuple-element.139, f32[1024,384]{1,0:T(8,128)} %get-tuple-element.116, ...), kind=kLoop, calls=%fused_computation.75 | loop fusion | flops 9829632 | bytes 8667648 | tf_op jit(solution)/shard_map/reduce_sum | solution.py:426
  102.2 1.4 copy.117
  104.7 1.0 fusion.92.mine
  105.7 8.5 %shard_map.283 = f32[6,64,128]{2,1,0:T(8,128)S(1)} custom-call(f32[6,64,128]{2,1,0:T(8,128)S(1)} %fusion.92.mine), custom_call_target="tpu_custom_call" | custom-call | tf_op jit(solution)/shard_map/pallas_call | solution.py:178
  114.7 1.5 fusion.42
  116.9 6.1 %fusion.3 = (f32[4,6,256]{2,1,0:T(8,128)S(1)}, f32[4,6,256]{2,1,0:T(8,128)S(1)}, f32[4,6,256]{2,1,0:T(8,128)S(1)}, f32[4,256,256]{2,1,0:T(8,128)}) fusion(f32[4,6,256]{2,1,0:T(8,128)S(1)} %bitcast.279, f32[4,6,256]{2,1,0:T(8,128)S(1)} %fusion.90, f32[4,256,256]{2,1,0:T(8,128)S(1)} %copy-done.40, pred[256,256]{1,0:T(8,128)(4,1)S(1)} %copy-done.44, ...), kind=kOutput, calls=%fused_computation.13 | convolution fusion | flops 221493248 | bytes 3858432 | tf_op jit(solution)/shard_map/cthp,cshp->chts/dot_general | solution.py:428
  123.7 1.9 fusion.130
  125.9 3.4 fusion.39
  129.3 1.0 copy.120
  130.3 1.5 copy.140
  131.8 1.9 copy.124
  133.8 2.0 convolution_bitcast_fusion.1
  135.8 1.0 convolution_add_fusion.1
  137.4 0.6 convolution_add_fusion
  138.1 47.3 %shard_map.284 = f32[1024,256]{1,0:T(8,128)S(1)} custom-call(f32[1024,256]{1,0:T(8,128)S(1)} %pad_maximum_fusion.2.part), custom_call_target="tpu_custom_call" | custom-call | tf_op jit(solution)/shard_map/pallas_call | solution.py:205
  185.4 3.2 multiply_reduce_fusion.5
  188.9 2.4 broadcast_multiply_fusion.3
  191.3 5.4 %shard_map.285 = f32[8,640]{1,0:T(8,128)S(1)} custom-call(f32[8,640]{1,0:T(8,128)S(1)} %pad_add_fusion.1.mine), custom_call_target="tpu_custom_call" | custom-call | tf_op jit(solution)/shard_map/pallas_call | solution.py:178
  196.7 0.8 pad_add_fusion
  197.8 0.9 copy-done.41
  198.7 2.4 convolution_convert_fusion
  201.0 1.2 copy-done.25
  202.4 1.0 slice.302
  203.6 4.2 %fusion.34.part = bf16[1024,768]{1,0:T(8,128)(2,1)S(1)} fusion(bf16[1024,384]{1,0:T(8,128)(2,1)} %get-tuple-element.123, bf16[1024,6]{1,0:T(8,128)(2,1)S(1)} %copy-done.42, bf16[1024,256]{1,0:T(8,128)(2,1)S(1)} %slice_select_fusion, bf16[1024,384]{1,0:T(8,128)(2,1)} %slice.302, bf16[768,1536]{1,0:T(8,128)(2,1)} %copy-done.2), kind=kOutput, calls=%fused_computation.59 | convolution fusion | flops 1824522240 | bytes 5451776 | tf_op jit(solution)/shard_map/dot_general | solution.py:283
  207.7 24.2 %shard_map.286 = bf16[1024,768]{1,0:T(8,128)(2,1)S(1)} custom-call(bf16[1024,768]{1,0:T(8,128)(2,1)S(1)} %fusion.34.part), custom_call_target="tpu_custom_call" | custom-call | tf_op jit(solution)/shard_map/pallas_call | solution.py:262
  231.9 1.4 fusion.15
  233.4 0.8 broadcast_in_dim.108
  234.2 2.0 fusion.60
  236.2 5.1 %concatenate.44.grads = bf16[768,1536]{1,0:T(8,128)(2,1)} concatenate(bf16[768,1030]{1,0:T(8,128)(2,1)} %bitcast.273, bf16[768,1]{1,0:T(8,128)(2,1)} %broadcast_in_dim.108, bf16[768,121]{1,0:T(8,128)(2,1)S(1)} %slice.305, bf16[768,384]{1,0:T(8,128)(2,1)} %fusion.60), dimensions={1} | concatenate | bytes 4718592 | tf_op jit(solution)/shard_map/concatenate | solution.py:502
  241.3 1.7 copy-done.1
  243.0 59.3 %shard_map.287 = (f32[48,1536]{1,0:T(8,128)S(1)}, f32[16,384]{1,0:T(8,128)S(1)}) custom-call(bf16[768,1536]{1,0:T(8,128)(2,1)S(1)} %copy-done.1, f32[16,384]{1,0:T(8,128)S(1)} %concatenate.46.small), custom_call_target="tpu_custom_call" | custom-call | tf_op jit(solution)/shard_map/pallas_call | solution.py:142
  302.3 0.7 slice_bitcast_fusion.8
  303.0 0.6 slice.264
  303.6 0.7 copy.129
  304.9 0.6 slice_reduce_fusion.5
  307.2 0.7 slice_reduce_fusion
  307.9 3.5 %fusion.8 = f32[1,1024,768]{2,1,0:T(8,128)} fusion(bf16[1024,768]{1,0:T(8,128)(2,1)S(1)} %shard_map.286, bf16[1,1024,768]{2,1,0:T(8,128)(2,1)} %param.31, f32[1024]{0:T(1024)S(1)} %broadcast_multiply_fusion.5, f32[1024]{0:T(1024)S(1)} %copy-done.48, f32[768]{0:T(1024)S(1)} %convert_reduce_fusion, f32[1024]{0:T(1024)S(1)} %get-tuple-element.142, ...), kind=kLoop, calls=%fused_computation.20 | loop fusion | flops 7077888 | bytes 7879680 | tf_op jit(solution)/shard_map/broadcast_in_dim | solution.py:501
  311.5 2.1 convolution_convert_fusion.1.part
  313.6 24.5 %shard_map.282 = bf16[1024,768]{1,0:T(8,128)(2,1)S(1)} custom-call(bf16[1024,768]{1,0:T(8,128)(2,1)S(1)} %convolution_convert_fusion.1.part, bf16[1024,768]{1,0:T(8,128)(2,1)S(1)} %bitcast.253), custom_call_target="tpu_custom_call" | custom-call | tf_op jit(solution)/shard_map/pallas_call | solution.py:262
  338.1 1.1 copy.173
  (206 shorter events, 12.1 us)
Async XLA Ops:
  0.6 46.9 %copy-start = (bf16[1,1024,768]{2,1,0:T(8,128)(2,1)S(1)}, bf16[1,1024,768]{2,1,0:T(8,128)(2,1)}, u32[]{:S(2)}) copy-start(bf16[1,1024,768]{2,1,0:T(8,128)(2,1)} %param.16) | copy-start | bytes 4718596
  44.3 5.6 %copy-start.2 = (bf16[768,1536]{1,0:T(8,128)(2,1)}, bf16[768,1536]{1,0:T(8,128)(2,1)S(1)}, u32[]{:S(2)}) copy-start(bf16[768,1536]{1,0:T(8,128)(2,1)S(1)} %get-tuple-element.21) | copy-start | bytes 7077892
  47.5 2.3 copy-start.63
  47.6 4.5 %copy-start.59 = (f32[6]{0:T(128)S(1)}, f32[6]{0:T(128)}, u32[]{:S(2)}) copy-start(f32[6]{0:T(128)} %param.27) | copy-start | bytes 76
  49.9 2.1 copy-start.15
  53.4 13.2 %copy-start.45 = (f32[4,256,6]{1,2,0:T(8,128)}, f32[4,256,6]{1,2,0:T(8,128)S(1)}, u32[]{:S(2)}) copy-start(f32[4,256,6]{1,2,0:T(8,128)S(1)} %bitcast_multiply_fusion.5) | copy-start | bytes 73732
  57.0 0.7 copy-start.61
  57.7 2.9 copy-start.3
  66.5 2.3 copy-start.11
  68.1 0.9 copy-start.19
  68.2 11.3 %copy-start.54 = (f32[6]{0:T(128)}, f32[6]{0:T(128)S(1)}, u32[]{:S(2)}) copy-start(f32[6]{0:T(128)S(1)} %get-tuple-element.145) | copy-start | bytes 76
  68.2 11.3 %copy-start.56 = (f32[6]{0:T(128)}, f32[6]{0:T(128)S(1)}, u32[]{:S(2)}) copy-start(f32[6]{0:T(128)S(1)} %get-tuple-element.148) | copy-start | bytes 76
  76.5 3.0 copy-start.12
  77.7 2.1 copy-start.16
  77.7 2.1 copy-start.26
  77.7 2.1 copy-start.29
  79.0 3.3 copy-start.32
  79.1 1.2 copy-start.20
  79.1 1.2 copy-start.65
  79.5 2.9 copy-start.8
  79.8 2.5 copy-start.39
  80.3 2.1 copy-start.43
  84.9 3.1 copy-start.49
  102.2 2.4 copy-start.55
  103.7 10.5 %copy-start.57 = (f32[6]{0:T(128)S(1)}, f32[6]{0:T(128)}, u32[]{:S(2)}) copy-start(f32[6]{0:T(128)} %copy-done.56) | copy-start | bytes 76
  104.3 21.7 %copy-start.22 = (bf16[4,256,6,64]{1,0,3,2:T(4,128)(2,1)}, bf16[4,256,6,64]{1,0,3,2:T(4,128)(2,1)S(1)}, u32[]{:S(2)}) copy-start(bf16[4,256,6,64]{1,0,3,2:T(4,128)(2,1)S(1)} %reshape.177) | copy-start | bytes 2359300
  104.3 10.2 %copy-start.17 = (f32[6,64,128]{2,1,0:T(8,128)S(1)}, f32[6,64,128]{2,1,0:T(8,128)}, u32[]{:S(2)}) copy-start(f32[6,64,128]{2,1,0:T(8,128)} %copy-done.16) | copy-start | bytes 589828
  104.3 10.2 %copy-start.27 = (f32[1,6,64,128]{3,2,1,0:T(8,128)S(1)}, f32[1,6,64,128]{3,2,1,0:T(8,128)}, u32[]{:S(2)}) copy-start(f32[1,6,64,128]{3,2,1,0:T(8,128)} %copy-done.26) | copy-start | bytes 589828
  104.3 10.2 %copy-start.30 = (f32[1,6,64,128]{3,2,1,0:T(8,128)S(1)}, f32[1,6,64,128]{3,2,1,0:T(8,128)}, u32[]{:S(2)}) copy-start(f32[1,6,64,128]{3,2,1,0:T(8,128)} %copy-done.29) | copy-start | bytes 589828
  104.3 10.2 %copy-start.33 = (f32[1,6,64,128]{3,2,1,0:T(8,128)S(1)}, f32[1,6,64,128]{3,2,1,0:T(8,128)}, u32[]{:S(2)}) copy-start(f32[1,6,64,128]{3,2,1,0:T(8,128)} %copy-done.32) | copy-start | bytes 589828
  104.7 10.0 %copy-start.13 = (bf16[1024,128]{1,0:T(8,128)(2,1)S(1)}, bf16[1024,128]{1,0:T(8,128)(2,1)}, u32[]{:S(2)}) copy-start(bf16[1024,128]{1,0:T(8,128)(2,1)} %copy-done.11) | copy-start | bytes 786436
  104.7 10.0 %copy-start.21 = (bf16[4,256,6,64]{1,0,3,2:T(4,128)(2,1)S(1)}, bf16[4,256,6,64]{1,0,3,2:T(4,128)(2,1)}, u32[]{:S(2)}) copy-start(bf16[4,256,6,64]{1,0,3,2:T(4,128)(2,1)} %reshape.170) | copy-start | bytes 2359300
  114.3 1.9 copy-start.24
  114.3 1.9 copy-start.36
  114.3 1.9 copy-start.37
  114.4 1.8 copy-start.35
  114.5 2.0 copy-start.9
  114.7 2.2 copy-start.40
  114.7 2.2 copy-start.44
  116.9 6.5 %copy-start.64 = (f32[6]{0:T(128)S(1)}, f32[6]{0:T(128)}, u32[]{:S(2)}) copy-start(f32[6]{0:T(128)} %param.28) | copy-start | bytes 76
  116.9 6.8 %copy-start.60 = (f32[6]{0:T(128)S(1)}, f32[6]{0:T(128)}, u32[]{:S(2)}) copy-start(f32[6]{0:T(128)} %param.27) | copy-start | bytes 76
  116.9 8.8 %copy-start.51 = (f32[384]{0:T(512)S(1)}, f32[384]{0:T(512)}, u32[]{:S(2)}) copy-start(f32[384]{0:T(512)} %get-tuple-element.109) | copy-start | bytes 4612
  116.9 9.1 %copy-start.46 = (f32[4,256,6]{1,2,0:T(8,128)S(1)}, f32[4,256,6]{1,2,0:T(8,128)}, u32[]{:S(2)}) copy-start(f32[4,256,6]{1,2,0:T(8,128)} %copy-done.45) | copy-start | bytes 73732
  116.9 9.1 %copy-start.66 = (f32[6]{0:T(128)S(1)}, f32[6]{0:T(128)}, u32[]{:S(2)}) copy-start(f32[6]{0:T(128)} %param.29) | copy-start | bytes 76
  131.8 1.9 copy-start.47
  133.7 2.1 copy-start.10
  133.7 3.1 copy-start.18
  133.7 3.1 copy-start.23
  133.7 3.1 copy-start.28
  133.8 3.1 copy-start.31
  133.8 3.1 copy-start.34
  135.8 1.6 copy-start.14
  137.4 48.0 %copy-start.5 = (f32[1024,640]{1,0:T(8,128)S(1)}, f32[1024,640]{1,0:T(8,128)}, u32[]{:S(2)}) copy-start(f32[1024,640]{1,0:T(8,128)} %get-tuple-element.122) | copy-start | bytes 7864324
  138.0 47.4 %copy-start.4 = (f32[1027,640]{1,0:T(8,128)S(1)}, f32[1027,640]{1,0:T(8,128)}, u32[]{:S(2)}) copy-start(f32[1027,640]{1,0:T(8,128)} %copy-done.3) | copy-start | bytes 7887364
  185.4 3.3 copy-start.52
  197.5 1.1 copy-start.41
  197.5 1.2 copy-start.42
  201.0 1.2 copy-start.25
  231.9 2.3 copy-start.6
  231.9 2.3 copy-start.38
  231.9 2.3 copy-start.50
  241.3 1.7 copy-start.1
  243.0 65.0 %copy-start.48 = (f32[1024]{0:T(1024)S(1)}, f32[1024]{0:T(1024)}, u32[]{:S(2)}) copy-start(f32[1024]{0:T(1024)} %get-tuple-element.141) | copy-start | bytes 12292
  307.9 3.5 %copy-start.7 = (f32[1024,384]{1,0:T(8,128)S(1)}, f32[1024,384]{1,0:T(8,128)}, u32[]{:S(2)}) copy-start(f32[1024,384]{1,0:T(8,128)} %get-tuple-element.116) | copy-start | bytes 4718596
  (3 other events, 2.1 us)
